TPU v7x, 32 devices: a whole 2x2x4 slice. The times are simulated.
32 devices in a mesh: row: 8 (over y, x, core), frame: 4 (over z).
Axes of the slice: x: 2, y: 2, z: 4, core: 2. Of those that a mesh axis runs over, the one named last changes fastest.
Arguments:
- frames: bfloat16 [16, 64, 64, 128], P('frame', None, 'row'), may hold values from -6 to 6
- w_pair: bfloat16 [3, 3, 64, 128], replicated, may hold values from -0.1875 to 0.1875
- w_mixed: bfloat16 [3, 3, 64, 64], replicated, may hold values from -0.25 to 0.25
- slope_pair: float32 [64], replicated, may hold values from 0.05 to 0.5
- slope_mixed: float32 [64], replicated, may hold values from 0.05 to 0.5
Outputs:
- merged: bfloat16 [4, 64, 64, 128], P('frame', None, 'row')
All inputs are finite; a program needn't handle non-finite values.
Results may differ from a plain program's by a relative error of at most 0.0051.
Values may be sent and summed in bfloat16 or wider, within the bound.
A program may use at most 64 MiB of HBM per device.

v0:
```python
import jax
import jax.numpy as jnp
from jax import lax
from jax.sharding import PartitionSpec as P


def padded_2(cells, sides, width):
    for axis, dim in sides:
        count = lax.axis_size(axis)
        ends = count - 1
        head = lax.slice_in_dim(cells, 0, width, axis=dim)
        tail = lax.slice_in_dim(cells, cells.shape[dim] - width, cells.shape[dim], axis=dim)
        cells = jnp.concatenate(
            [
                lax.ppermute(tail, axis, [(i, (i + 1) % count) for i in range(ends)]),
                cells,
                lax.ppermute(head, axis, [((i + 1) % count, i) for i in range(ends)]),
            ],
            axis=dim,
        )
    return cells


def swapped(block, axis, bit):
    count = lax.axis_size(axis)
    route = []
    for low in range(count):
        high = low | 1 << bit
        if high != low and high < count:
            route += [(low, high), (high, low)]
    return lax.ppermute(block, axis, route)


def prelu(values, slope):
    return jnp.where(values >= 0, values, slope[None, :, None, None] * values)


def convolve(padded, weight):
    out_rows = padded.shape[2] - 2
    cols = padded.shape[3]
    wide = jnp.pad(padded, ((0, 0), (0, 0), (0, 0), (1, 1)))
    total = jnp.zeros((padded.shape[0], weight.shape[2], out_rows, cols), jnp.float32)
    for tap_y in range(3):
        for tap_x in range(3):
            total = total + jnp.einsum(
                "oc,fchw->fohw",
                weight[tap_y, tap_x],
                wide[:, :, tap_y : tap_y + out_rows, tap_x : tap_x + cols],
                preferred_element_type=jnp.float32,
            )
    return total


def merge_block(first, second, w_pair, w_mixed, slope_pair, slope_mixed):
    joined = jnp.concatenate([first, second], axis=1)
    padded = padded_2(joined, (("row", 2),), 1)
    hidden = prelu(convolve(padded, w_pair), slope_pair).astype(jnp.bfloat16)
    padded_hidden = padded_2(hidden, (("row", 2),), 1)
    branch = prelu(convolve(padded_hidden, w_mixed), slope_mixed)
    return (first.astype(jnp.float32) + branch).astype(jnp.bfloat16)


def on_device(frames, w_pair, w_mixed, slope_pair, slope_mixed):
    count = lax.axis_size("frame")
    place = lax.axis_index("frame")
    top_bit = count.bit_length() - 2
    next_bit = top_bit - 1
    quarter = count // 4
    upper = place >= count // 2
    high = place // quarter % 2 == 1

    def merge(first, second):
        return merge_block(first, second, w_pair, w_mixed, slope_pair, slope_mixed)

    outgoing = jnp.where(upper, frames[0:2], frames[2:4])
    partner = swapped(outgoing, "frame", top_bit)
    level_one = merge(
        jnp.where(upper, partner, frames[0:2]), jnp.where(upper, frames[2:4], partner)
    )
    outgoing_one = jnp.where(high, level_one[0:1], level_one[1:2])
    partner_one = swapped(outgoing_one, "frame", next_bit)
    merged = merge(
        jnp.where(high, partner_one, level_one[0:1]), jnp.where(high, level_one[1:2], partner_one)
    )
    return merged


def solution(mesh):
    placed = (P("frame", None, "row", None), P(), P(), P(), P())
    return jax.shard_map(
        on_device,
        mesh=mesh,
        in_specs=placed,
        out_specs=P("frame", None, "row", None),
        check_vma=False,
    )
```

profile of v0, /device:TPU:1, one launch (start us, length us, event | category | flops | bytes accessed | tf_op | source)
XLA Modules:
  0.0 66.5 jit_solution(2552244861723737161)
XLA Ops:
  0.0 1.1 %fusion.170 = (bf16[2,64,8,128]{3,2,1,0:T(8,128)(2,1)S(1)}, bf16[2,64,8,128]{3,2,1,0:T(8,128)(2,1)S(1)}) fusion(bf16[4,64,8,128]{3,2,1,0:T(8,128)(2,1)} %param.5), kind=kLoop, calls=%fused_computation.240 | loop fusion | bytes 1048576 | tf_op jit(solution)/shard_map/slice | solution.py:75
  1.1 0.0 copy-start.1
  1.1 0.1 broadcast_select_fusion.2
  1.2 3.2 %collective-permute-start = (bf16[2,64,8,128]{3,1,2,0:T(8,128)(2,1)S(1)}, bf16[2,64,8,128]{3,1,2,0:T(8,128)(2,1)S(1)}, u32[]{:S(2)}, u32[]{:S(2)}) collective-permute-start(bf16[2,64,8,128]{3,1,2,0:T(8,128)(2,1)S(1)} %broadcast_select_fusion.2), channel_id=1, source_target_pairs={{0,2},{2,0},{1,3},{3,1},{4,6},{6,4},{5,7},{7,5},{8,10},{10,8},{9,1... | collective-permute-start | bytes 786440 | tf_op jit(solution)/shard_map/ppermute | solution.py:31
  4.4 11.6 %collective-permute-done = bf16[2,64,8,128]{3,1,2,0:T(8,128)(2,1)S(1)} collective-permute-done((bf16[2,64,8,128]{3,1,2,0:T(8,128)(2,1)S(1)}, bf16[2,64,8,128]{3,1,2,0:T(8,128)(2,1)S(1)}, u32[]{:S(2)}, u32[]{:S(2)}) %collective-permute-start) | collective-permute-done | bytes 262176 | tf_op jit(solution)/shard_map/ppermute | solution.py:31
  16.0 0.1 broadcast_select_fusion
  16.1 4.3 %collective-permute-start.1 = (bf16[2,128,1,128]{3,1,2,0:T(8,128)(2,1)S(1)}, bf16[2,128,1,128]{3,1,2,0:T(8,128)(2,1)S(1)}, u32[]{:S(2)}, u32[]{:S(2)}) collective-permute-start(bf16[2,128,1,128]{3,1,2,0:T(8,128)(2,1)S(1)} %get-tuple-element.5), channel_id=1, source_target_pairs={{0,4},{4,8},{8,12},{12,16},{16,20},{20,24},{24,28},{1,5},{5,9},{9,... | collective-permute-start | bytes 196616 | tf_op jit(solution)/shard_map/ppermute | solution.py:15
  20.4 1.9 %collective-permute-start.2 = (bf16[2,128,1,128]{3,1,2,0:T(8,128)(2,1)S(1)}, bf16[2,128,1,128]{3,1,2,0:T(8,128)(2,1)S(1)}, u32[]{:S(2)}, u32[]{:S(2)}) collective-permute-start(bf16[2,128,1,128]{3,1,2,0:T(8,128)(2,1)S(1)} %get-tuple-element.6), channel_id=1, source_target_pairs={{4,0},{8,4},{12,8},{16,12},{20,16},{24,20},{28,24},{5,1},{9,5},{13... | collective-permute-start | bytes 196616 | tf_op jit(solution)/shard_map/ppermute | solution.py:17
  22.3 0.2 fusion.45
  22.6 3.4 %collective-permute-done.2 = bf16[2,128,1,128]{3,1,2,0:T(8,128)(2,1)S(1)} collective-permute-done((bf16[2,128,1,128]{3,1,2,0:T(8,128)(2,1)S(1)}, bf16[2,128,1,128]{3,1,2,0:T(8,128)(2,1)S(1)}, u32[]{:S(2)}, u32[]{:S(2)}) %collective-permute-start.2) | collective-permute-done | bytes 65568 | tf_op jit(solution)/shard_map/ppermute | solution.py:17
  26.0 0.8 %select_maximum_fusion = bf16[2,128,10,130]{3,1,2,0:T(8,128)(2,1)S(1)} fusion(bf16[2,128,1,128]{3,1,2,0:T(8,128)(2,1)S(1)} %collective-permute-done.2, bf16[2,128,1,128]{3,1,2,0:T(8,128)(2,1)S(1)} %collective-permute-done.1, bf16[2,64,8,128]{3,1,2,0:T(8,128)(2,1)S(1)} %get-tuple-element.15, bf16[2,64,8,128]{3,1,2,0:T(8,128)(2,1)S(1)} %get-tuple-element.16), kind=kLoop, calls=%fused_computation.9 | loop fusion | flops 4992000 | bytes 1320960 | tf_op jit(solution)/shard_map/concatenate | solution.py:13
  26.7 0.2 fusion.34
  27.0 0.4 fusion.36
  27.4 0.2 fusion.38
  27.6 0.4 fusion.40
  28.0 0.4 fusion.30
  28.4 0.2 fusion.32
  28.6 0.2 fusion.42
  28.8 0.2 copy-done.3
  29.0 0.5 fusion.20
  29.5 1.9 %collective-permute-start.3 = (bf16[2,64,1,128]{3,1,2,0:T(8,128)(2,1)S(1)}, bf16[2,64,1,128]{3,1,2,0:T(8,128)(2,1)S(1)}, u32[]{:S(2)}, u32[]{:S(2)}) collective-permute-start(bf16[2,64,1,128]{3,1,2,0:T(8,128)(2,1)S(1)} %get-tuple-element.13), channel_id=1, source_target_pairs={{0,4},{4,8},{8,12},{12,16},{16,20},{20,24},{24,28},{1,5},{5,9},{9,... | collective-permute-start | bytes 98312 | tf_op jit(solution)/shard_map/ppermute | solution.py:15
  31.4 2.4 %collective-permute-start.4 = (bf16[2,64,1,128]{3,1,2,0:T(8,128)(2,1)S(1)}, bf16[2,64,1,128]{3,1,2,0:T(8,128)(2,1)S(1)}, u32[]{:S(2)}, u32[]{:S(2)}) collective-permute-start(bf16[2,64,1,128]{3,1,2,0:T(8,128)(2,1)S(1)} %get-tuple-element.14), channel_id=1, source_target_pairs={{4,0},{8,4},{12,8},{16,12},{20,16},{24,20},{28,24},{5,1},{9,5},{13... | collective-permute-start | bytes 98312 | tf_op jit(solution)/shard_map/ppermute | solution.py:17
  33.9 3.6 %collective-permute-done.4 = bf16[2,64,1,128]{3,1,2,0:T(8,128)(2,1)S(1)} collective-permute-done((bf16[2,64,1,128]{3,1,2,0:T(8,128)(2,1)S(1)}, bf16[2,64,1,128]{3,1,2,0:T(8,128)(2,1)S(1)}, u32[]{:S(2)}, u32[]{:S(2)}) %collective-permute-start.4) | collective-permute-done | bytes 32800 | tf_op jit(solution)/shard_map/ppermute | solution.py:17
  37.4 0.3 fusion.25
  37.8 0.3 fusion.65
  38.0 0.2 fusion.72
  38.3 0.2 convolution_add_fusion.6
  38.5 0.3 convolution_add_fusion.5
  38.8 0.2 convolution_add_fusion.4
  39.0 0.2 convolution_add_fusion.3
  39.2 0.0 copy-start.2
  39.2 0.3 convolution_add_fusion.2
  39.5 0.2 convolution_add_fusion.1
  39.7 0.1 copy-done.2
  39.9 0.3 add_convert_fusion
  40.2 0.5 collective-permute-start.5
  40.6 3.4 %collective-permute-done.5 = bf16[1,64,8,128]{3,1,2,0:T(8,128)(2,1)S(1)} collective-permute-done((bf16[1,64,8,128]{3,1,2,0:T(8,128)(2,1)S(1)}, bf16[1,64,8,128]{3,1,2,0:T(8,128)(2,1)S(1)}, u32[]{:S(2)}, u32[]{:S(2)}) %collective-permute-start.5) | collective-permute-done | bytes 131104 | tf_op jit(solution)/shard_map/ppermute | solution.py:31
  44.1 3.1 %collective-permute-start.6 = (bf16[1,128,1,128]{3,1,2,0:T(8,128)(2,1)S(1)}, bf16[1,128,1,128]{3,1,2,0:T(8,128)(2,1)S(1)}, u32[]{:S(2)}, u32[]{:S(2)}) collective-permute-start(bf16[1,128,1,128]{3,1,2,0:T(8,128)(2,1)S(1)} %get-tuple-element.11), channel_id=1, source_target_pairs={{0,4},{4,8},{8,12},{12,16},{16,20},{20,24},{24,28},{1,5},{5,9},{9,... | collective-permute-start | bytes 98312 | tf_op jit(solution)/shard_map/ppermute | solution.py:15
  47.2 1.9 %collective-permute-start.7 = (bf16[1,128,1,128]{3,1,2,0:T(8,128)(2,1)S(1)}, bf16[1,128,1,128]{3,1,2,0:T(8,128)(2,1)S(1)}, u32[]{:S(2)}, u32[]{:S(2)}) collective-permute-start(bf16[1,128,1,128]{3,1,2,0:T(8,128)(2,1)S(1)} %get-tuple-element.12), channel_id=1, source_target_pairs={{4,0},{8,4},{12,8},{16,12},{20,16},{24,20},{28,24},{5,1},{9,5},{13... | collective-permute-start | bytes 98312 | tf_op jit(solution)/shard_map/ppermute | solution.py:17
  49.1 3.3 %collective-permute-done.7 = bf16[1,128,1,128]{3,1,2,0:T(8,128)(2,1)S(1)} collective-permute-done((bf16[1,128,1,128]{3,1,2,0:T(8,128)(2,1)S(1)}, bf16[1,128,1,128]{3,1,2,0:T(8,128)(2,1)S(1)}, u32[]{:S(2)}, u32[]{:S(2)}) %collective-permute-start.7) | collective-permute-done | bytes 32800 | tf_op jit(solution)/shard_map/ppermute | solution.py:17
  52.4 0.3 select_maximum_fusion.2
  52.7 0.2 fusion.64
  52.9 0.3 fusion.57
  53.2 0.2 convolution_add_fusion.21
  53.4 0.3 convolution_add_fusion.20
  53.7 0.2 convolution_add_fusion.19
  53.8 0.2 convolution_add_fusion.18
  54.0 0.3 convolution_add_fusion.17
  54.3 0.2 convolution_add_fusion.16
  54.5 0.2 fusion.49
  54.7 2.2 %collective-permute-start.8 = (bf16[1,64,1,128]{3,1,2,0:T(8,128)(2,1)S(1)}, bf16[1,64,1,128]{3,1,2,0:T(8,128)(2,1)S(1)}, u32[]{:S(2)}, u32[]{:S(2)}) collective-permute-start(bf16[1,64,1,128]{3,1,2,0:T(8,128)(2,1)S(1)} %get-tuple-element.17), channel_id=1, source_target_pairs={{0,4},{4,8},{8,12},{12,16},{16,20},{20,24},{24,28},{1,5},{5,9},{9,... | collective-permute-start | bytes 49160 | tf_op jit(solution)/shard_map/ppermute | solution.py:15
  56.9 2.2 %collective-permute-start.9 = (bf16[1,64,1,128]{3,1,2,0:T(8,128)(2,1)S(1)}, bf16[1,64,1,128]{3,1,2,0:T(8,128)(2,1)S(1)}, u32[]{:S(2)}, u32[]{:S(2)}) collective-permute-start(bf16[1,64,1,128]{3,1,2,0:T(8,128)(2,1)S(1)} %get-tuple-element.18), channel_id=1, source_target_pairs={{4,0},{8,4},{12,8},{16,12},{20,16},{24,20},{28,24},{5,1},{9,5},{13... | collective-permute-start | bytes 49160 | tf_op jit(solution)/shard_map/ppermute | solution.py:17
  59.1 4.7 %collective-permute-done.9 = bf16[1,64,1,128]{3,1,2,0:T(8,128)(2,1)S(1)} collective-permute-done((bf16[1,64,1,128]{3,1,2,0:T(8,128)(2,1)S(1)}, bf16[1,64,1,128]{3,1,2,0:T(8,128)(2,1)S(1)}, u32[]{:S(2)}, u32[]{:S(2)}) %collective-permute-start.9) | collective-permute-done | bytes 16416 | tf_op jit(solution)/shard_map/ppermute | solution.py:17
  63.7 0.2 fusion.54
  63.9 0.2 fusion.84
  64.1 0.2 fusion.75
  64.3 0.2 convolution_add_fusion.14
  64.5 0.2 convolution_add_fusion.13
  64.8 0.2 convolution_add_fusion.12
  64.9 0.2 convolution_add_fusion.11
  65.1 0.2 convolution_add_fusion.10
  65.4 0.2 convolution_add_fusion.9
  65.5 0.2 add_convert_fusion.1
  65.8 0.7 %copy.8 = bf16[1,64,8,128]{3,2,1,0:T(8,128)(2,1)} copy(bf16[1,64,8,128]{3,1,2,0:T(8,128)(2,1)S(1)} %add_convert_fusion.1) | data formatting | bytes 262144 | tf_op jit(solution)/shard_map/convert_element_type | solution.py:60
  (14 shorter events, 0.1 us)
Async XLA Ops:
  1.1 21.3 %copy-start.1 = (bf16[3,3,64,128]{3,2,1,0:T(8,128)(2,1)S(1)}, bf16[3,3,64,128]{3,2,1,0:T(8,128)(2,1)}, u32[]{:S(2)}) copy-start(bf16[3,3,64,128]{3,2,1,0:T(8,128)(2,1)} %param.6) | copy-start | bytes 442372
  1.2 14.9 %collective-permute-start = (bf16[2,64,8,128]{3,1,2,0:T(8,128)(2,1)S(1)}, bf16[2,64,8,128]{3,1,2,0:T(8,128)(2,1)S(1)}, u32[]{:S(2)}, u32[]{:S(2)}) collective-permute-start(bf16[2,64,8,128]{3,1,2,0:T(8,128)(2,1)S(1)} %broadcast_select_fusion.2), channel_id=1, source_target_pairs={{0,2},{2,0},{1,3},{3,1},{4,6},{6,4},{5,7},{7,5},{8,10},{10,8},{9,1... | collective-permute-start | bytes 786440 | tf_op jit(solution)/shard_map/ppermute | solution.py:31
  16.1 6.5 %collective-permute-start.1 = (bf16[2,128,1,128]{3,1,2,0:T(8,128)(2,1)S(1)}, bf16[2,128,1,128]{3,1,2,0:T(8,128)(2,1)S(1)}, u32[]{:S(2)}, u32[]{:S(2)}) collective-permute-start(bf16[2,128,1,128]{3,1,2,0:T(8,128)(2,1)S(1)} %get-tuple-element.5), channel_id=1, source_target_pairs={{0,4},{4,8},{8,12},{12,16},{16,20},{20,24},{24,28},{1,5},{5,9},{9,... | collective-permute-start | bytes 196616 | tf_op jit(solution)/shard_map/ppermute | solution.py:15
  20.4 5.6 %collective-permute-start.2 = (bf16[2,128,1,128]{3,1,2,0:T(8,128)(2,1)S(1)}, bf16[2,128,1,128]{3,1,2,0:T(8,128)(2,1)S(1)}, u32[]{:S(2)}, u32[]{:S(2)}) collective-permute-start(bf16[2,128,1,128]{3,1,2,0:T(8,128)(2,1)S(1)} %get-tuple-element.6), channel_id=1, source_target_pairs={{4,0},{8,4},{12,8},{16,12},{20,16},{24,20},{28,24},{5,1},{9,5},{13... | collective-permute-start | bytes 196616 | tf_op jit(solution)/shard_map/ppermute | solution.py:17
  28.4 0.7 copy-start.3
  29.0 8.7 %copy-start = (bf16[3,3,64,64]{3,2,1,0:T(8,128)(2,1)S(1)}, bf16[3,3,64,64]{3,2,1,0:T(8,128)(2,1)}, u32[]{:S(2)}) copy-start(bf16[3,3,64,64]{3,2,1,0:T(8,128)(2,1)} %param.7) | copy-start | bytes 221188
  29.5 4.4 %collective-permute-start.3 = (bf16[2,64,1,128]{3,1,2,0:T(8,128)(2,1)S(1)}, bf16[2,64,1,128]{3,1,2,0:T(8,128)(2,1)S(1)}, u32[]{:S(2)}, u32[]{:S(2)}) collective-permute-start(bf16[2,64,1,128]{3,1,2,0:T(8,128)(2,1)S(1)} %get-tuple-element.13), channel_id=1, source_target_pairs={{0,4},{4,8},{8,12},{12,16},{16,20},{20,24},{24,28},{1,5},{5,9},{9,... | collective-permute-start | bytes 98312 | tf_op jit(solution)/shard_map/ppermute | solution.py:15
  31.4 6.0 %collective-permute-start.4 = (bf16[2,64,1,128]{3,1,2,0:T(8,128)(2,1)S(1)}, bf16[2,64,1,128]{3,1,2,0:T(8,128)(2,1)S(1)}, u32[]{:S(2)}, u32[]{:S(2)}) collective-permute-start(bf16[2,64,1,128]{3,1,2,0:T(8,128)(2,1)S(1)} %get-tuple-element.14), channel_id=1, source_target_pairs={{4,0},{8,4},{12,8},{16,12},{20,16},{24,20},{28,24},{5,1},{9,5},{13... | collective-permute-start | bytes 98312 | tf_op jit(solution)/shard_map/ppermute | solution.py:17
  39.2 0.7 copy-start.2
  40.2 3.9 %collective-permute-start.5 = (bf16[1,64,8,128]{3,1,2,0:T(8,128)(2,1)S(1)}, bf16[1,64,8,128]{3,1,2,0:T(8,128)(2,1)S(1)}, u32[]{:S(2)}, u32[]{:S(2)}) collective-permute-start(bf16[1,64,8,128]{3,1,2,0:T(8,128)(2,1)S(1)} %broadcast_select_fusion.5), channel_id=1, source_target_pairs={{0,1},{1,0},{2,3},{3,2},{4,5},{5,4},{6,7},{7,6},{8,9},{9,8},{10,11... | collective-permute-start | bytes 393224 | tf_op jit(solution)/shard_map/ppermute | solution.py:31
  44.1 5.0 %collective-permute-start.6 = (bf16[1,128,1,128]{3,1,2,0:T(8,128)(2,1)S(1)}, bf16[1,128,1,128]{3,1,2,0:T(8,128)(2,1)S(1)}, u32[]{:S(2)}, u32[]{:S(2)}) collective-permute-start(bf16[1,128,1,128]{3,1,2,0:T(8,128)(2,1)S(1)} %get-tuple-element.11), channel_id=1, source_target_pairs={{0,4},{4,8},{8,12},{12,16},{16,20},{20,24},{24,28},{1,5},{5,9},{9,... | collective-permute-start | bytes 98312 | tf_op jit(solution)/shard_map/ppermute | solution.py:15
  47.2 5.2 %collective-permute-start.7 = (bf16[1,128,1,128]{3,1,2,0:T(8,128)(2,1)S(1)}, bf16[1,128,1,128]{3,1,2,0:T(8,128)(2,1)S(1)}, u32[]{:S(2)}, u32[]{:S(2)}) collective-permute-start(bf16[1,128,1,128]{3,1,2,0:T(8,128)(2,1)S(1)} %get-tuple-element.12), channel_id=1, source_target_pairs={{4,0},{8,4},{12,8},{16,12},{20,16},{24,20},{28,24},{5,1},{9,5},{13... | collective-permute-start | bytes 98312 | tf_op jit(solution)/shard_map/ppermute | solution.py:17
  54.7 4.3 %collective-permute-start.8 = (bf16[1,64,1,128]{3,1,2,0:T(8,128)(2,1)S(1)}, bf16[1,64,1,128]{3,1,2,0:T(8,128)(2,1)S(1)}, u32[]{:S(2)}, u32[]{:S(2)}) collective-permute-start(bf16[1,64,1,128]{3,1,2,0:T(8,128)(2,1)S(1)} %get-tuple-element.17), channel_id=1, source_target_pairs={{0,4},{4,8},{8,12},{12,16},{16,20},{20,24},{24,28},{1,5},{5,9},{9,... | collective-permute-start | bytes 49160 | tf_op jit(solution)/shard_map/ppermute | solution.py:15
  56.9 6.9 %collective-permute-start.9 = (bf16[1,64,1,128]{3,1,2,0:T(8,128)(2,1)S(1)}, bf16[1,64,1,128]{3,1,2,0:T(8,128)(2,1)S(1)}, u32[]{:S(2)}, u32[]{:S(2)}) collective-permute-start(bf16[1,64,1,128]{3,1,2,0:T(8,128)(2,1)S(1)} %get-tuple-element.18), channel_id=1, source_target_pairs={{4,0},{8,4},{12,8},{16,12},{20,16},{24,20},{28,24},{5,1},{9,5},{13... | collective-permute-start | bytes 49160 | tf_op jit(solution)/shard_map/ppermute | solution.py:17
where the time goes:
time: 67 us; the launch traced here: 66.5 us
  waiting for transfers between devices  30 us (45%)
  starting transfers between devices  23.5 us (35%)
  matrix products  8.59 us (13%)
  local copies, waits for them, and re-layouts  2.17 us (3%)
  other arithmetic  1.76 us (3%)
    ppermute x2, waiting for transfers between devices, swapped(): return lax.ppermute(block, axis, route)  15.1 us
    ppermute x4, waiting for transfers between devices, padded_2(): lax.ppermute(head, axis, [((i + 1) % count, i) for i in range(ends)])  14.9 us
    ppermute x4, starting transfers between devices, padded_2(): lax.ppermute(tail, axis, [(i, (i + 1) % count) for i in range(ends)])  11.4 us
    dot_general x36, matrix products, convolve(): jnp.einsum('oc,fchw->fohw', weight[tap_y, tap_x], wide[:, :, tap_y:tap_y...  8.59 us
    ppermute x4, starting transfers between devices, padded_2(): lax.ppermute(head, axis, [((i + 1) % count, i) for i in range(ends)])  8.4 us
    ppermute x2, starting transfers between devices, swapped(): return lax.ppermute(block, axis, route)  3.66 us
    concatenate x4, other arithmetic, padded_2(): jnp.concatenate([lax.ppermute(tail, axis, [(i, (i + 1) % count) for i in...  1.57 us
  transfers between devices with their start and end apart: 10, of which 6 were waited for; matrix products, arithmetic and copies ran while one was open for 0% of the time, Pallas kernels for 0%

commit v1 on v0

v1 whole, which is shorter than its diff:
```python
import functools

import jax
import jax.numpy as jnp
from jax import lax
from jax.experimental import pallas as pl
from jax.experimental.pallas import tpu as pltpu
from jax.sharding import PartitionSpec as P

HALO = 4
GROUP = 4
TILE = 2


def spread(slope_ref, channels, cols):
    row = jnp.broadcast_to(slope_ref[...], (cols, channels))
    return row.T


def kernel(
    rows,
    cols,
    x_ref,
    w_pair_ref,
    w_mixed_ref,
    slope_pair_ref,
    slope_mixed_ref,
    out_ref,
    buf,
    acc,
    hidden,
    one,
    acc_two,
    wp,
    wm,
    sp,
    sm,
    send_z,
    recv_z,
    send_h,
    recv_h,
    own_sem,
):
    channels = x_ref.shape[1]
    row = lax.axis_index("row")
    place = lax.axis_index("frame")
    row_count = lax.axis_size("row")
    n = lax.axis_size("frame") // GROUP
    k = place // n
    m = place % n
    near = k + 1 - 2 * (k % 2)
    across = (k + 2) % GROUP
    far = GROUP - 1 - k
    has_up = row > 0
    has_down = row < row_count - 1
    edge = HALO * cols
    block = rows * cols

    def device(slot):
        return (row, slot * n + m)

    up = (row - 1, place)
    down = (row + 1, place)

    barrier = pltpu.get_barrier_semaphore()
    for slot in (near, across, far):
        pl.semaphore_signal(barrier, inc=1, device_id=device(slot), device_id_type=pl.DeviceIdType.MESH)

    @pl.when(has_up)
    def _():
        pl.semaphore_signal(barrier, inc=1, device_id=up, device_id_type=pl.DeviceIdType.MESH)

    @pl.when(has_down)
    def _():
        pl.semaphore_signal(barrier, inc=1, device_id=down, device_id_type=pl.DeviceIdType.MESH)

    pl.semaphore_wait(barrier, 3 + has_up.astype(jnp.int32) + has_down.astype(jnp.int32))

    def z_copy(slot):
        return pltpu.make_async_remote_copy(
            src_ref=x_ref.at[slot],
            dst_ref=buf.at[k, :, edge : edge + block],
            send_sem=send_z.at[slot],
            recv_sem=recv_z.at[k],
            device_id=device(slot),
            device_id_type=pl.DeviceIdType.MESH,
        )

    def z_arrival(slot):
        return pltpu.make_async_remote_copy(
            src_ref=x_ref.at[slot],
            dst_ref=buf.at[slot, :, edge : edge + block],
            send_sem=send_z.at[slot],
            recv_sem=recv_z.at[slot],
            device_id=device(slot),
            device_id_type=pl.DeviceIdType.MESH,
        )

    for slot in (far, across, near):
        z_copy(slot).start()

    def halo_up(slot):
        return pltpu.make_async_remote_copy(
            src_ref=buf.at[slot, :, edge : 2 * edge],
            dst_ref=buf.at[slot, :, edge + block : 2 * edge + block],
            send_sem=send_h.at[slot, 0],
            recv_sem=recv_h.at[slot, 0],
            device_id=up,
            device_id_type=pl.DeviceIdType.MESH,
        )

    def halo_down(slot):
        return pltpu.make_async_remote_copy(
            src_ref=buf.at[slot, :, block : block + edge],
            dst_ref=buf.at[slot, :, 0:edge],
            send_sem=send_h.at[slot, 1],
            recv_sem=recv_h.at[slot, 1],
            device_id=down,
            device_id_type=pl.DeviceIdType.MESH,
        )

    def forward(slot):
        @pl.when(has_up)
        def _():
            halo_up(slot).start()

        @pl.when(has_down)
        def _():
            halo_down(slot).start()

    def halo_wait(slot):
        @pl.when(has_up)
        def _():
            halo_down(slot).wait_recv()

        @pl.when(has_down)
        def _():
            halo_up(slot).wait_recv()

    own = pltpu.make_async_copy(x_ref.at[k], buf.at[k, :, edge : edge + block], own_sem)
    own.start()

    @pl.when(jnp.logical_not(has_up))
    def _():
        buf[:, :, 0:edge] = jnp.zeros((GROUP, channels, edge), buf.dtype)

    @pl.when(jnp.logical_not(has_down))
    def _():
        buf[:, :, edge + block : 2 * edge + block] = jnp.zeros((GROUP, channels, edge), buf.dtype)

    own.wait()
    forward(k)

    for kx in range(3):
        for part in range(2):
            wp[part, kx * channels : (kx + 1) * channels, :] = jnp.concatenate(
                [w_pair_ref[ky, kx][:, part * channels : (part + 1) * channels] for ky in range(3)], axis=1
            )
        wm[kx * channels : (kx + 1) * channels, :] = jnp.concatenate([w_mixed_ref[ky, kx] for ky in range(3)], axis=1)
    sp[...] = spread(slope_pair_ref, channels, cols)
    sm[...] = spread(slope_mixed_ref, channels, cols)

    lane = lax.broadcasted_iota(jnp.int32, (channels, cols), 1)
    not_first = lane > 0
    not_last = lane < cols - 1

    def tiles(count):
        return [(at, min(TILE, count - at)) for at in range(0, count, TILE)]

    def taps(weight, source, at, size):
        stacked = jnp.concatenate(
            [source[:, (at + ky) * cols : (at + ky + size) * cols] for ky in range(3)], axis=0
        )
        return jnp.dot(weight, stacked, preferred_element_type=jnp.float32)

    def joined(partial, i):
        left = partial[0:channels, i * cols : (i + 1) * cols]
        middle = partial[channels : 2 * channels, i * cols : (i + 1) * cols]
        right = partial[2 * channels :, i * cols : (i + 1) * cols]
        return (
            middle
            + jnp.where(not_first, pltpu.roll(left, 1, 1), 0.0)
            + jnp.where(not_last, pltpu.roll(right, cols - 1, 1), 0.0)
        )

    def prelu(values, slope):
        return jnp.where(values >= 0, values, slope[...] * values)

    def inside(values, image_row):
        if image_row < 0:
            return jnp.where(has_up, values, 0.0)
        if image_row >= rows:
            return jnp.where(has_down, values, 0.0)
        return values

    def begin(weight, source, target, reach):
        for at, size in tiles(rows + 2 * reach):
            target[:, at * cols : (at + size) * cols] = taps(weight, source, at, size)

    def merge(weight, source, started, first, first_reach, reach, target):
        for at, size in tiles(rows + 2 * reach + 2):
            partial = started[:, at * cols : (at + size) * cols] + taps(weight, source, at, size)
            for i in range(size):
                value = inside(prelu(joined(partial, i), sp), at + i - reach - 1)
                hidden[:, (at + i) * cols : (at + i + 1) * cols] = value.astype(hidden.dtype)
        weight_two = wm[...]
        for at, size in tiles(rows + 2 * reach):
            partial = taps(weight_two, hidden, at, size)
            for i in range(size):
                from_row = at + i - reach + first_reach
                base = first[:, from_row * cols : (from_row + 1) * cols].astype(jnp.float32)
                value = inside(base + prelu(joined(partial, i), sm), at + i - reach)
                target[:, (at + i) * cols : (at + i + 1) * cols] = value.astype(target.dtype)

    half = GROUP // 2

    def begin_pair(slot):
        begin(wp[slot // half], buf.at[slot], acc.at[slot % half], 3)

    def finish_pair(slot):
        pair = slot % half
        merge(wp[slot // half], buf.at[slot], acc.at[pair], buf.at[pair], HALO, 2, one.at[pair])

    halo_wait(k)
    begin_pair(k)
    z_arrival(near).wait_recv()
    forward(near)
    halo_wait(near)
    begin_pair(near)
    z_arrival(across).wait_recv()
    forward(across)
    z_arrival(far).wait_recv()
    forward(far)
    halo_wait(across)
    finish_pair(across)
    begin(wp[k % half], one.at[k % half], acc_two, 1)
    halo_wait(far)
    finish_pair(far)
    merge(wp[near % half], one.at[near % half], acc_two, one.at[0], 2, 0, out_ref)

    for slot in (near, across, far):
        z_copy(slot).wait_send()
    for slot in range(GROUP):
        @pl.when(has_up)
        def _():
            halo_up(slot).wait_send()

        @pl.when(has_down)
        def _():
            halo_down(slot).wait_send()


def on_device(frames, w_pair, w_mixed, slope_pair, slope_mixed):
    slots, channels, rows, cols = frames.shape
    x = frames.reshape(slots, channels, rows * cols)
    vmem = pl.BlockSpec(memory_space=pltpu.VMEM)
    wide = (rows + 2 * HALO) * cols
    merged = pl.pallas_call(
        functools.partial(kernel, rows, cols),
        out_shape=jax.ShapeDtypeStruct((channels, rows * cols), frames.dtype),
        in_specs=[vmem] * 5,
        out_specs=vmem,
        scratch_shapes=[
            pltpu.VMEM((GROUP, channels, wide), frames.dtype),
            pltpu.VMEM((2, 3 * channels, wide - 2 * cols), jnp.float32),
            pltpu.VMEM((channels, wide - 2 * cols), frames.dtype),
            pltpu.VMEM((2, channels, wide - 4 * cols), frames.dtype),
            pltpu.VMEM((3 * channels, wide - 6 * cols), jnp.float32),
            pltpu.VMEM((2, 3 * channels, 3 * channels), w_pair.dtype),
            pltpu.VMEM((3 * channels, 3 * channels), w_pair.dtype),
            pltpu.VMEM((channels, cols), jnp.float32),
            pltpu.VMEM((channels, cols), jnp.float32),
            pltpu.SemaphoreType.DMA((GROUP,)),
            pltpu.SemaphoreType.DMA((GROUP,)),
            pltpu.SemaphoreType.DMA((GROUP, 2)),
            pltpu.SemaphoreType.DMA((GROUP, 2)),
            pltpu.SemaphoreType.DMA,
        ],
        compiler_params=pltpu.CompilerParams(
            collective_id=0, has_side_effects=True, vmem_limit_bytes=32 * 1024 * 1024
        ),
    )(x, w_pair, w_mixed, slope_pair.reshape(1, channels), slope_mixed.reshape(1, channels))
    return merged.reshape(1, channels, rows, cols)


def solution(mesh):
    placed = (P("frame", None, "row", None), P(), P(), P(), P())
    return jax.shard_map(
        on_device,
        mesh=mesh,
        in_specs=placed,
        out_specs=P("frame", None, "row", None),
        check_vma=False,
    )
```

time: 67 us -> 25.9 us (0.39)
  waiting for transfers between devices: 30 us -> 0 us
  Pallas kernels: 0 us -> 23.7 us
  starting transfers between devices: 23.5 us -> 0 us
  matrix products: 8.59 us -> 0 us
  other arithmetic: 1.76 us -> 0 us
    ppermute x10 -> x0, waiting for transfers between devices: 30 us -> none  [the longest x2 15.1 us: swapped(): return lax.ppermute(block, axis, route)]
    pallas_call x0 -> x1, Pallas kernels: none -> 23.7 us  [on_device(): pl.pallas_call(functools.partial(kernel, rows, cols), out_shape=jax.Shape...]
    ppermute x10 -> x0, starting transfers between devices: 23.5 us -> none  [the longest x4 11.4 us: padded_2(): lax.ppermute(tail, axis, [(i, (i + 1) % count) for i in range(ends)])]
    dot_general x36 -> x0, matrix products: 8.59 us -> none  [convolve(): jnp.einsum('oc,fchw->fohw', weight[tap_y, tap_x], wide[:, :, tap_y:tap_y...]
    concatenate x5 -> x0, other arithmetic: 1.57 us -> none  [the longest x4 1.57 us: padded_2(): jnp.concatenate([lax.ppermute(tail, axis, [(i, (i + 1) % count) for i in...]
    reshape x0 -> x1, local copies, waits for them, and re-layouts: none -> 1.31 us  [on_device(): x = frames.reshape(slots, channels, rows * cols)]
    slice x3 -> x0, local copies, waits for them, and re-layouts: 1.08 us -> none  [the longest x1 1.06 us: on_device(): outgoing = jnp.where(upper, frames[0:2], frames[2:4])]
    convert_element_type x1 -> x0, local copies, waits for them, and re-layouts: 0.74 us -> none  [merge_block(): return (first.astype(jnp.float32) + branch).astype(jnp.bfloat16)]
  transfers between devices with their start and end apart: 10 -> 0, of which waited for: 6 -> 0; matrix products, arithmetic and copies ran while one was open for 0% -> 0% of each run, Pallas kernels for 0% -> 0%
where the time goes in v1:
time: 25.9 us; the launch traced here: 25.8 us
  Pallas kernels  23.7 us (92%)
  local copies, waits for them, and re-layouts  2 us (8%)
    pallas_call x1, Pallas kernels, on_device(): pl.pallas_call(functools.partial(kernel, rows, cols), out_shape=jax.Shape...  23.7 us
    reshape x1, local copies, waits for them, and re-layouts, on_device(): x = frames.reshape(slots, channels, rows * cols)  1.31 us
    unnamed x9, local copies, waits for them, and re-layouts  0.69 us

profile of v1, /device:TPU:1, one launch (start us, length us, event | category | flops | bytes accessed | tf_op | source)
XLA Modules:
  0.0 25.8 jit_solution(11697453586379138088)
XLA Ops:
  0.0 0.0 copy-start
  0.0 0.0 copy-start.1
  0.0 0.0 copy-start.2
  0.0 0.0 copy-start.3
  0.0 1.3 %reshape.12.x_ref = bf16[4,64,1024]{2,1,0:T(8,128)(2,1)S(1)} reshape(bf16[4,64,8,128]{3,2,1,0:T(8,128)(2,1)} %param.5) | data formatting | bytes 1048576 | tf_op jit(solution)/shard_map/reshape | solution.py:255
  1.3 0.0 copy-done
  1.3 0.0 copy-done.1
  1.4 0.0 copy-done.2
  1.4 0.0 copy-done.3
  1.4 23.7 %shard_map.55 = bf16[64,1024]{1,0:T(8,128)(2,1)S(1)} custom-call(bf16[4,64,1024]{2,1,0:T(8,128)(2,1)S(1)} %reshape.12.x_ref, bf16[3,3,64,128]{3,2,1,0:T(8,128)(2,1)S(1)} %copy-done, bf16[3,3,64,64]{3,2,1,0:T(8,128)(2,1)S(1)} %copy-done.1, f32[1,64]{1,0:T(1,128)S(1)} %bitcast.8, f32[1,64]{1,0:T(1,128)S(1)} %bitcast.9), custom_call_target="tpu_custom_call" | custom-call | tf_op jit(solution)/shard_map/pallas_call | solution.py:258
  25.1 0.7 %copy.6 = bf16[8,8,8,128]{3,2,1,0:T(8,128)(2,1)} copy(bf16[8,8,8,128]{3,1,2,0:T(8,128)(2,1)S(1)} %bitcast.7) | data formatting | bytes 262144
Async XLA Ops:
  0.0 1.3 %copy-start = (bf16[3,3,64,128]{3,2,1,0:T(8,128)(2,1)S(1)}, bf16[3,3,64,128]{3,2,1,0:T(8,128)(2,1)}, u32[]{:S(2)}) copy-start(bf16[3,3,64,128]{3,2,1,0:T(8,128)(2,1)} %w_pair_ref.1) | copy-start | bytes 442372
  0.0 1.3 %copy-start.1 = (bf16[3,3,64,64]{3,2,1,0:T(8,128)(2,1)S(1)}, bf16[3,3,64,64]{3,2,1,0:T(8,128)(2,1)}, u32[]{:S(2)}) copy-start(bf16[3,3,64,64]{3,2,1,0:T(8,128)(2,1)} %w_mixed_ref.1) | copy-start | bytes 221188
  0.0 1.3 %copy-start.2 = (f32[64]{0:T(128)S(1)}, f32[64]{0:T(128)}, u32[]{:S(2)}) copy-start(f32[64]{0:T(128)} %param.8) | copy-start | bytes 772
  0.0 1.4 %copy-start.3 = (f32[64]{0:T(128)S(1)}, f32[64]{0:T(128)}, u32[]{:S(2)}) copy-start(f32[64]{0:T(128)} %param.9) | copy-start | bytes 772

commit v2 on v1

v2 whole, which is shorter than its diff:
```python
import functools

import jax
import jax.numpy as jnp
from jax import lax
from jax.experimental import pallas as pl
from jax.experimental.pallas import tpu as pltpu
from jax.sharding import PartitionSpec as P

HALO = 4
GROUP = 4
TILE = 2
PIECES = 2


def spread(slope_ref, channels, cols):
    row = jnp.broadcast_to(slope_ref[...], (cols, channels))
    return row.T


def kernel(
    rows,
    cols,
    x_ref,
    w_pair_ref,
    w_mixed_ref,
    slope_pair_ref,
    slope_mixed_ref,
    out_ref,
    raw,
    x,
    w_pair_in,
    w_mixed_in,
    slope_pair_in,
    slope_mixed_in,
    buf,
    acc,
    hidden,
    one,
    acc_two,
    wp,
    wm,
    sp,
    sm,
    send_z,
    recv_z,
    send_h,
    recv_h,
    in_sem,
    w_sem,
):
    channels = x_ref.shape[1]
    row = lax.axis_index("row")
    place = lax.axis_index("frame")
    row_count = lax.axis_size("row")
    n = lax.axis_size("frame") // GROUP
    k = place // n
    m = place % n
    near = k + 1 - 2 * (k % 2)
    across = (k + 2) % GROUP
    far = GROUP - 1 - k
    has_up = row > 0
    has_down = row < row_count - 1
    edge = HALO
    deep = rows // PIECES

    def device(slot):
        return (row, slot * n + m)

    up = (row - 1, place)
    down = (row + 1, place)

    def fetch(slot):
        return pltpu.make_async_copy(x_ref.at[slot], raw.at[slot], in_sem.at[slot])

    def turned(slot):
        fetch(slot).wait()
        return jnp.swapaxes(raw[slot], 0, 1)

    loads = [
        pltpu.make_async_copy(source, target, w_sem.at[i])
        for i, (source, target) in enumerate(
            (
                (w_pair_ref, w_pair_in),
                (w_mixed_ref, w_mixed_in),
                (slope_pair_ref, slope_pair_in),
                (slope_mixed_ref, slope_mixed_in),
            )
        )
    ]
    for slot in (near, across, far, k):
        fetch(slot).start()

    barrier = pltpu.get_barrier_semaphore()
    for slot in (near, across, far):
        pl.semaphore_signal(barrier, inc=1, device_id=device(slot), device_id_type=pl.DeviceIdType.MESH)

    @pl.when(has_up)
    def _():
        pl.semaphore_signal(barrier, inc=1, device_id=up, device_id_type=pl.DeviceIdType.MESH)

    @pl.when(has_down)
    def _():
        pl.semaphore_signal(barrier, inc=1, device_id=down, device_id_type=pl.DeviceIdType.MESH)

    for load in loads:
        load.start()
    for slot in (near, across, far):
        x[slot] = turned(slot)
    pl.semaphore_wait(barrier, 3 + has_up.astype(jnp.int32) + has_down.astype(jnp.int32))

    def z_copy(slot, piece):
        return pltpu.make_async_remote_copy(
            src_ref=x.at[slot, piece * deep : (piece + 1) * deep],
            dst_ref=buf.at[k, edge + piece * deep : edge + (piece + 1) * deep],
            send_sem=send_z.at[slot, piece],
            recv_sem=recv_z.at[k, piece],
            device_id=device(slot),
            device_id_type=pl.DeviceIdType.MESH,
        )

    def z_arrival(slot, piece):
        return pltpu.make_async_remote_copy(
            src_ref=x.at[slot, piece * deep : (piece + 1) * deep],
            dst_ref=buf.at[slot, edge + piece * deep : edge + (piece + 1) * deep],
            send_sem=send_z.at[slot, piece],
            recv_sem=recv_z.at[slot, piece],
            device_id=device(slot),
            device_id_type=pl.DeviceIdType.MESH,
        )

    for piece in range(PIECES):
        for slot in (near, across, far):
            z_copy(slot, piece).start()

    def halo_up(slot):
        return pltpu.make_async_remote_copy(
            src_ref=buf.at[slot, edge : 2 * edge],
            dst_ref=buf.at[slot, edge + rows : 2 * edge + rows],
            send_sem=send_h.at[slot, 0],
            recv_sem=recv_h.at[slot, 0],
            device_id=up,
            device_id_type=pl.DeviceIdType.MESH,
        )

    def halo_down(slot):
        return pltpu.make_async_remote_copy(
            src_ref=buf.at[slot, rows : rows + edge],
            dst_ref=buf.at[slot, 0:edge],
            send_sem=send_h.at[slot, 1],
            recv_sem=recv_h.at[slot, 1],
            device_id=down,
            device_id_type=pl.DeviceIdType.MESH,
        )

    def forward(slot, piece):
        if piece == 0:
            @pl.when(has_up)
            def _():
                halo_up(slot).start()

        if piece == PIECES - 1:
            @pl.when(has_down)
            def _():
                halo_down(slot).start()

    def pass_on(slot, piece):
        z_arrival(slot, piece).wait_recv()
        forward(slot, piece)

    def halo_wait(slot):
        @pl.when(has_up)
        def _():
            halo_down(slot).wait_recv()

        @pl.when(has_down)
        def _():
            halo_up(slot).wait_recv()

    buf[k, edge : edge + rows] = turned(k)
    for piece in range(PIECES):
        forward(k, piece)

    @pl.when(jnp.logical_not(has_up))
    def _():
        buf[:, 0:edge] = jnp.zeros((GROUP, edge, channels, cols), buf.dtype)

    @pl.when(jnp.logical_not(has_down))
    def _():
        buf[:, edge + rows :] = jnp.zeros((GROUP, edge, channels, cols), buf.dtype)

    for load in loads:
        load.wait()

    for kx in range(3):
        for part in range(2):
            wp[part, kx * channels : (kx + 1) * channels, :] = jnp.concatenate(
                [w_pair_in[ky, kx][:, part * channels : (part + 1) * channels] for ky in range(3)], axis=1
            )
        wm[kx * channels : (kx + 1) * channels, :] = jnp.concatenate([w_mixed_in[ky, kx] for ky in range(3)], axis=1)
    sp[...] = spread(slope_pair_in, channels, cols)
    sm[...] = spread(slope_mixed_in, channels, cols)

    lane = lax.broadcasted_iota(jnp.int32, (channels, cols), 1)
    not_first = lane > 0
    not_last = lane < cols - 1

    def tiles(count):
        return [(at, min(TILE, count - at)) for at in range(0, count, TILE)]

    def taps(weight, source, at, size):
        lines = [source[at + i] for i in range(size + 2)]
        stacked = jnp.concatenate(
            [jnp.concatenate(lines[ky : ky + size], axis=1) for ky in range(3)], axis=0
        )
        return jnp.dot(weight, stacked, preferred_element_type=jnp.float32)

    def joined(partial, i):
        left = partial[0:channels, i * cols : (i + 1) * cols]
        middle = partial[channels : 2 * channels, i * cols : (i + 1) * cols]
        right = partial[2 * channels :, i * cols : (i + 1) * cols]
        return (
            middle
            + jnp.where(not_first, pltpu.roll(left, 1, 1), 0.0)
            + jnp.where(not_last, pltpu.roll(right, cols - 1, 1), 0.0)
        )

    def prelu(values, slope):
        return jnp.where(values >= 0, values, slope[...] * values)

    def inside(values, image_row):
        if image_row < 0:
            return jnp.where(has_up, values, 0.0)
        if image_row >= rows:
            return jnp.where(has_down, values, 0.0)
        return values

    def begin(weight, source, target, reach):
        for at, size in tiles(rows + 2 * reach):
            target[:, at * cols : (at + size) * cols] = taps(weight, source, at, size)

    def merge(weight, source, started, first, first_reach, reach, target):
        for at, size in tiles(rows + 2 * reach + 2):
            partial = started[:, at * cols : (at + size) * cols] + taps(weight, source, at, size)
            for i in range(size):
                value = inside(prelu(joined(partial, i), sp), at + i - reach - 1)
                hidden[at + i] = value.astype(hidden.dtype)
        weight_two = wm[...]
        for at, size in tiles(rows + 2 * reach):
            partial = taps(weight_two, hidden, at, size)
            for i in range(size):
                from_row = at + i - reach + first_reach
                base = first[from_row].astype(jnp.float32)
                value = inside(base + prelu(joined(partial, i), sm), at + i - reach)
                target[at + i] = value.astype(target.dtype)

    half = GROUP // 2

    def begin_pair(slot):
        begin(wp[slot // half], buf.at[slot], acc.at[slot % half], 3)

    def finish_pair(slot):
        pair = slot % half
        merge(wp[slot // half], buf.at[slot], acc.at[pair], buf.at[pair], HALO, 2, one.at[pair])

    halo_wait(k)
    begin_pair(k)
    for piece in range(PIECES - 1):
        for slot in (near, across, far):
            pass_on(slot, piece)
    pass_on(near, PIECES - 1)
    halo_wait(near)
    begin_pair(near)
    for slot in (across, far):
        pass_on(slot, PIECES - 1)
    halo_wait(across)
    finish_pair(across)
    begin(wp[k % half], one.at[k % half], acc_two, 1)
    halo_wait(far)
    finish_pair(far)
    merge(wp[near % half], one.at[near % half], acc_two, one.at[0], 2, 0, out_ref)

    for piece in range(PIECES):
        for slot in (near, across, far):
            z_copy(slot, piece).wait_send()
    for slot in range(GROUP):
        @pl.when(has_up)
        def _():
            halo_up(slot).wait_send()

        @pl.when(has_down)
        def _():
            halo_down(slot).wait_send()


def on_device(frames, w_pair, w_mixed, slope_pair, slope_mixed):
    slots, channels, rows, cols = frames.shape
    assert rows >= 2 * HALO
    slope_shape = (1, channels)
    vmem = pl.BlockSpec(memory_space=pltpu.VMEM)
    tall = rows + 2 * HALO
    merged = pl.pallas_call(
        functools.partial(kernel, rows, cols),
        out_shape=jax.ShapeDtypeStruct((rows, channels, cols), frames.dtype),
        in_specs=[pl.BlockSpec(memory_space=pltpu.HBM)] * 5,
        out_specs=vmem,
        scratch_shapes=[
            pltpu.VMEM(frames.shape, frames.dtype),
            pltpu.VMEM((slots, rows, channels, cols), frames.dtype),
            pltpu.VMEM(w_pair.shape, w_pair.dtype),
            pltpu.VMEM(w_mixed.shape, w_mixed.dtype),
            pltpu.VMEM(slope_shape, slope_pair.dtype),
            pltpu.VMEM(slope_shape, slope_mixed.dtype),
            pltpu.VMEM((GROUP, tall, channels, cols), frames.dtype),
            pltpu.VMEM((2, 3 * channels, (tall - 2) * cols), jnp.float32),
            pltpu.VMEM((tall - 2, channels, cols), frames.dtype),
            pltpu.VMEM((2, tall - 4, channels, cols), frames.dtype),
            pltpu.VMEM((3 * channels, (tall - 6) * cols), jnp.float32),
            pltpu.VMEM((2, 3 * channels, 3 * channels), w_pair.dtype),
            pltpu.VMEM((3 * channels, 3 * channels), w_pair.dtype),
            pltpu.VMEM((channels, cols), jnp.float32),
            pltpu.VMEM((channels, cols), jnp.float32),
            pltpu.SemaphoreType.DMA((GROUP, PIECES)),
            pltpu.SemaphoreType.DMA((GROUP, PIECES)),
            pltpu.SemaphoreType.DMA((GROUP, 2)),
            pltpu.SemaphoreType.DMA((GROUP, 2)),
            pltpu.SemaphoreType.DMA((GROUP,)),
            pltpu.SemaphoreType.DMA((4,)),
        ],
        compiler_params=pltpu.CompilerParams(
            collective_id=0, has_side_effects=True, vmem_limit_bytes=60 * 1024 * 1024
        ),
    )(frames, w_pair, w_mixed, slope_pair.reshape(slope_shape), slope_mixed.reshape(slope_shape))
    return merged.transpose(1, 0, 2)[None]


def solution(mesh):
    placed = (P("frame", None, "row", None), P(), P(), P(), P())
    return jax.shard_map(
        on_device,
        mesh=mesh,
        in_specs=placed,
        out_specs=P("frame", None, "row", None),
        check_vma=False,
    )
```

time: 25.9 us -> 22.9 us (0.88)
  Pallas kernels: 23.7 us -> 21.1 us
  local copies, waits for them, and re-layouts: 2 us -> 1.65 us
    pallas_call x1, Pallas kernels: 23.7 us -> 21.1 us  [on_device(): pl.pallas_call(functools.partial(kernel, rows, cols), out_shape=jax.Shape...]
    broadcast_in_dim x0 -> x1, local copies, waits for them, and re-layouts: none -> 1.65 us  [on_device(): return merged.transpose(1, 0, 2)[None]]
    reshape x1 -> x0, local copies, waits for them, and re-layouts: 1.31 us -> none  [on_device(): x = frames.reshape(slots, channels, rows * cols)]
    unnamed x9 -> x0, local copies, waits for them, and re-layouts: 0.69 us -> none
where the time goes in v2:
time: 22.9 us; the launch traced here: 22.7 us
  Pallas kernels  21.1 us (92%)
  local copies, waits for them, and re-layouts  1.65 us (7%)
    pallas_call x1, Pallas kernels, on_device(): pl.pallas_call(functools.partial(kernel, rows, cols), out_shape=jax.Shape...  21.1 us
    broadcast_in_dim x1, local copies, waits for them, and re-layouts, on_device(): return merged.transpose(1, 0, 2)[None]  1.65 us

profile of v2, /device:TPU:1, one launch (start us, length us, event | category | flops | bytes accessed | tf_op | source)
XLA Modules:
  0.0 22.7 jit_solution(18331863740811377282)
XLA Ops:
  0.0 21.1 %shard_map.55 = bf16[8,64,128]{2,1,0:T(8,128)(2,1)} custom-call(bf16[4,64,8,128]{3,2,1,0:T(8,128)(2,1)} %x_ref.1, bf16[3,3,64,128]{3,2,1,0:T(8,128)(2,1)} %w_pair_ref.1, bf16[3,3,64,64]{3,2,1,0:T(8,128)(2,1)} %w_mixed_ref.1, f32[1,64]{1,0:T(1,128)} %bitcast.6, f32[1,64]{1,0:T(1,128)} %bitcast.7), custom_call_target="tpu_custom_call" | custom-call | tf_op jit(solution)/shard_map/pallas_call | solution.py:302
  21.1 1.6 %copy.6 = bf16[1,64,8,128]{3,2,1,0:T(8,128)(2,1)} copy(bf16[1,64,8,128]{3,1,2,0:T(8,128)(2,1)} %bitcast.5) | data formatting | bytes 262144 | tf_op jit(solution)/shard_map/broadcast_in_dim | solution.py:334

commit v3 on v2

--- a/solution.py
+++ b/solution.py
@@ -107,6 +107,7 @@
         load.start()
     for slot in (near, across, far):
         x[slot] = turned(slot)
+    buf[k, edge : edge + rows] = turned(k)
     pl.semaphore_wait(barrier, 3 + has_up.astype(jnp.int32) + has_down.astype(jnp.int32))
 
     def z_copy(slot, piece):
@@ -129,9 +130,6 @@
             device_id_type=pl.DeviceIdType.MESH,
         )
 
-    for piece in range(PIECES):
-        for slot in (near, across, far):
-            z_copy(slot, piece).start()
 
     def halo_up(slot):
         return pltpu.make_async_remote_copy(
@@ -177,9 +175,14 @@
         def _():
             halo_up(slot).wait_recv()
 
-    buf[k, edge : edge + rows] = turned(k)
+    for piece in range(1):
+        for slot in (near, across, far):
+            z_copy(slot, piece).start()
     for piece in range(PIECES):
         forward(k, piece)
+    for piece in range(1, PIECES):
+        for slot in (near, across, far):
+            z_copy(slot, piece).start()
 
     @pl.when(jnp.logical_not(has_up))
     def _():

time: 22.9 us -> 22.9 us (level)
  no operation moved by 1% of the time
where the time goes in v3:
time: 22.9 us; the launch traced here: 22.7 us
  Pallas kernels  21.1 us (92%)
  local copies, waits for them, and re-layouts  1.65 us (7%)
    pallas_call x1, Pallas kernels, on_device(): pl.pallas_call(functools.partial(kernel, rows, cols), out_shape=jax.Shape...  21.1 us
    broadcast_in_dim x1, local copies, waits for them, and re-layouts, on_device(): return merged.transpose(1, 0, 2)[None]  1.65 us

profile of v3, /device:TPU:1, one launch (start us, length us, event | category | flops | bytes accessed | tf_op | source)
XLA Modules:
  0.0 22.7 jit_solution(12240021227320312576)
XLA Ops:
  0.0 21.1 %shard_map.55 = bf16[8,64,128]{2,1,0:T(8,128)(2,1)} custom-call(bf16[4,64,8,128]{3,2,1,0:T(8,128)(2,1)} %x_ref.1, bf16[3,3,64,128]{3,2,1,0:T(8,128)(2,1)} %w_pair_ref.1, bf16[3,3,64,64]{3,2,1,0:T(8,128)(2,1)} %w_mixed_ref.1, f32[1,64]{1,0:T(1,128)} %bitcast.6, f32[1,64]{1,0:T(1,128)} %bitcast.7), custom_call_target="tpu_custom_call" | custom-call | tf_op jit(solution)/shard_map/pallas_call | solution.py:305
  21.1 1.6 %copy.6 = bf16[1,64,8,128]{3,2,1,0:T(8,128)(2,1)} copy(bf16[1,64,8,128]{3,1,2,0:T(8,128)(2,1)} %bitcast.5) | data formatting | bytes 262144 | tf_op jit(solution)/shard_map/broadcast_in_dim | solution.py:337
